TPU v7x, 128 devices: a whole 4x4x4 slice. The times are simulated.
128 devices in a mesh: blk: 4 (over x_lo, core), dom: 32 (over z, y, x_hi).
Axes of the slice: x: 4 (x_hi: 2, x_lo: 2; x = x_hi * 2 + x_lo), y: 4, z: 4, core: 2. Of those that a mesh axis runs over, the one named last changes fastest.
Arguments:
- node_feats: bfloat16 [65536, 512], P(('blk', 'dom')), may hold values from -6 to 6
- send_rows: int32 [128, 32, 32], P(('blk', 'dom')), may hold values from 0 to 511
- neighbour_slots: int32 [65536, 8], P(('blk', 'dom')), may hold values from 0 to 1535
- slot_mask: int32 [65536, 8], P(('blk', 'dom')), may hold values 0 or 1
- gate_weight: bfloat16 [512, 512], replicated, may hold values from -0.25 to 0.25
- source_weight: bfloat16 [512, 1024], replicated, may hold values from -0.25 to 0.25
- qkv_weight: bfloat16 [512, 1536], replicated, may hold values from -0.26516504 to 0.26516504
- out_weight: bfloat16 [512, 512], replicated, may hold values from -0.25 to 0.25
- cotangent: bfloat16 [65536, 512], P(('blk', 'dom')), may hold values from -6 to 6
Outputs:
- layer_out: bfloat16 [65536, 512], P(('blk', 'dom'))
- feats_grad: bfloat16 [65536, 512], P(('blk', 'dom'))
- gate_grad: float32 [512, 512], replicated
- source_grad: float32 [512, 1024], replicated
- qkv_grad: float32 [512, 1536], replicated
- out_grad: float32 [512, 512], replicated
Inputs may be any that keep to these rules, and one draw needn't show every extreme that they name: `send_rows`: local node indices of the sending device. `neighbour_slots`: rows below 512 are the device's own nodes, the others received rows.
All inputs are finite; a program needn't handle non-finite values. No bound on the sum of `slot_mask` on one device may be relied on, other than what follows from the above.
Results may differ from a plain program's by a relative error of at most 0.035.
Values may be sent and summed in bfloat16 or wider, within the bound.
No kernel may reach another device: no remote copies, remote signals or barrier semaphores. Data moves between devices by JAX's collectives and lax.ppermute only.
A program may use at most 256 MiB of HBM per device.

v0:
```python
import math
import jax
import jax.numpy as jnp
from jax import lax
from jax.sharding import PartitionSpec as P

HEADS = 8
HDIM = 64


def body(
    node_feats,
    send_rows,
    neighbour_slots,
    slot_mask,
    gate_weight,
    source_weight,
    qkv_weight,
    out_weight,
    cotangent,
):
    node_count, feat_width = node_feats.shape
    head_count = HEADS
    head_width = HDIM
    score_scale = 1.0 / math.sqrt(HDIM)
    peer_count = lax.axis_size("dom")
    outgoing = node_feats[send_rows[0]]
    incoming = lax.all_to_all(outgoing, "dom", split_axis=0, concat_axis=0, tiled=True)
    table = jnp.concatenate([node_feats, incoming.reshape(-1, feat_width)], axis=0)
    table_rows = table.shape[0]
    gate_term = jnp.dot(node_feats, gate_weight, preferred_element_type=jnp.float32)
    source_terms = jnp.dot(table, source_weight, preferred_element_type=jnp.float32)
    edge_source = source_terms[neighbour_slots]
    gate_open = jax.nn.sigmoid(gate_term[:, None, :] + edge_source[:, :, :feat_width])
    edge_value = edge_source[:, :, feat_width:]
    mask_float = slot_mask.astype(jnp.float32)
    slot_weight = mask_float / jnp.maximum(jnp.sum(mask_float, axis=1, keepdims=True), 1.0)
    message = jnp.sum(slot_weight[:, :, None] * gate_open * edge_value, axis=1)
    qkv = jnp.dot(node_feats, qkv_weight, preferred_element_type=jnp.float32).astype(jnp.bfloat16)
    queries = qkv[:, :feat_width].reshape(node_count, head_count, head_width)
    keys_vals = lax.all_gather(qkv[:, feat_width:], "blk", axis=0, tiled=True)
    seq_len = keys_vals.shape[0]
    all_keys = keys_vals[:, :feat_width].reshape(seq_len, head_count, head_width)
    all_values = keys_vals[:, feat_width:].reshape(seq_len, head_count, head_width)
    scores = (
        jnp.einsum("ihe,jhe->hij", queries, all_keys, preferred_element_type=jnp.float32)
        * score_scale
    )
    row_top = jnp.max(scores, axis=2, keepdims=True)
    raw_weights = jnp.exp(scores - row_top)
    row_total = jnp.sum(raw_weights, axis=2, keepdims=True)
    prob_weights = raw_weights / row_total
    prob_half = prob_weights.astype(jnp.bfloat16)
    mixed = (
        jnp.einsum("hij,jhe->ihe", prob_half, all_values, preferred_element_type=jnp.float32)
        .astype(jnp.bfloat16)
        .reshape(node_count, feat_width)
    )
    attended = jnp.dot(mixed, out_weight, preferred_element_type=jnp.float32)
    layer_out = (node_feats.astype(jnp.float32) + message + attended).astype(jnp.bfloat16)
    upstream = cotangent.astype(jnp.float32)
    grad_out_w = jnp.einsum("nd,ne->de", mixed, cotangent, preferred_element_type=jnp.float32)
    d_mixed = jnp.einsum(
        "ne,de->nd", cotangent, out_weight, preferred_element_type=jnp.float32
    ).astype(jnp.bfloat16)
    d_heads = d_mixed.reshape(node_count, head_count, head_width)
    row_delta = jnp.sum(
        d_heads.astype(jnp.float32)
        * mixed.reshape(node_count, head_count, head_width).astype(jnp.float32),
        axis=2,
    )
    d_probs = jnp.einsum("ihe,jhe->hij", d_heads, all_values, preferred_element_type=jnp.float32)
    d_scores = (prob_weights * (d_probs - row_delta.T[:, :, None]) * score_scale).astype(
        jnp.bfloat16
    )
    d_query = jnp.einsum(
        "hij,jhe->ihe", d_scores, all_keys, preferred_element_type=jnp.float32
    ).reshape(node_count, feat_width)
    count = node_count * lax.axis_size("blk")
    d_key = jnp.einsum("hij,ihe->jhe", d_scores, queries, preferred_element_type=jnp.float32)
    d_value = jnp.einsum("hij,ihe->jhe", prob_half, d_heads, preferred_element_type=jnp.float32)
    d_keyval = lax.psum_scatter(
        jnp.concatenate(
            [d_key.reshape(count, feat_width), d_value.reshape(count, feat_width)], axis=1
        ),
        "blk",
        scatter_dimension=0,
        tiled=True,
    )
    d_qkv = jnp.concatenate([d_query, d_keyval], axis=1).astype(jnp.bfloat16)
    grad_qkv_w = jnp.einsum("nd,nf->df", node_feats, d_qkv, preferred_element_type=jnp.float32)
    d_attn_input = jnp.einsum("nf,df->nd", d_qkv, qkv_weight, preferred_element_type=jnp.float32)
    edge_up = slot_weight[:, :, None] * upstream[:, None, :]
    d_edge_value = edge_up * gate_open
    d_edge_logit = edge_up * edge_value * gate_open * (1.0 - gate_open)
    d_gate = jnp.sum(d_edge_logit, axis=1).astype(jnp.bfloat16)
    edge_terms = jnp.concatenate([d_edge_logit, d_edge_value], axis=2).reshape(-1, 2 * feat_width)
    d_source = jax.ops.segment_sum(
        edge_terms, neighbour_slots.reshape(-1), num_segments=table_rows
    ).astype(jnp.bfloat16)
    grad_source_w = jnp.einsum("td,tf->df", table, d_source, preferred_element_type=jnp.float32)
    grad_gate_w = jnp.einsum("nd,nf->df", node_feats, d_gate, preferred_element_type=jnp.float32)
    d_table = jnp.einsum("tf,df->td", d_source, source_weight, preferred_element_type=jnp.float32)
    returned = lax.all_to_all(
        d_table[node_count:].reshape(peer_count, -1, feat_width).astype(jnp.bfloat16),
        "dom",
        split_axis=0,
        concat_axis=0,
        tiled=True,
    ).astype(jnp.float32)
    d_sent = jax.ops.segment_sum(
        returned.reshape(-1, feat_width), send_rows[0].reshape(-1), num_segments=node_count
    )
    d_gate_input = jnp.einsum("nf,df->nd", d_gate, gate_weight, preferred_element_type=jnp.float32)
    feats_grad = (upstream + d_attn_input + d_table[:node_count] + d_gate_input + d_sent).astype(
        jnp.bfloat16
    )
    weight_sums = lax.psum((grad_gate_w, grad_source_w, grad_qkv_w, grad_out_w), ("blk", "dom"))
    return (layer_out, feats_grad, weight_sums[0], weight_sums[1], weight_sums[2], weight_sums[3])


def solution(mesh):
    return jax.shard_map(
        body,
        mesh=mesh,
        in_specs=(
            P(("blk", "dom"), None),
            P(("blk", "dom"), None, None),
            P(("blk", "dom"), None),
            P(("blk", "dom"), None),
            P(),
            P(),
            P(),
            P(),
            P(("blk", "dom"), None),
        ),
        out_specs=(P(("blk", "dom"), None), P(("blk", "dom"), None), P(), P(), P(), P()),
        check_vma=False,
    )
```

profile of v0, /device:TPU:1, one launch (start us, length us, event | category | flops | bytes accessed | tf_op | source)
XLA Modules:
  0.0 508.1 jit_solution(13844792690348114465)
XLA Ops:
  7.2 0.0 all-gather.2.cloned.1.call-start
  7.2 1.3 copy-done
  8.6 2.0 convolution_convert_fusion
  10.6 1.1 copy-done.9
  11.8 1.1 slice.39
  12.8 0.0 all-gather.2.cloned.1.call-update
  12.9 0.0 reduce-scatter.2.cloned.1.call-start
  12.9 1.1 slice.41
  14.0 1.0 copy.27
  15.0 0.5 convolution_convert_fusion.1
  15.5 47.7 %all-gather.2.cloned.1.call-done = bf16[2048,1024]{1,0:T(8,128)(2,1)} async-done(((bf16[512,1024]{1,0:T(8,128)(2,1)}), bf16[2048,1024]{1,0:T(8,128)(2,1)}) %all-gather.2.cloned.1.call-update) | async-done | bytes 4194320 | tf_op jit(solution)/shard_map/all_gather | solution.py:41
  63.2 4.5 fusion.36
  67.7 4.0 copy.28
  71.7 3.9 copy.26
  75.6 16.6 %fusion.37 = (f32[8,512]{1,0:T(8,128)S(1)}, f32[8,512,2048]{2,1,0:T(8,128)}) fusion(bf16[512,8,64]{0,2,1:T(8,128)(2,1)S(1)} %bitcast.82, bf16[2048,8,64]{0,2,1:T(8,128)(2,1)} %bitcast.71), kind=kOutput, calls=%fused_computation.67 | convolution fusion | flops 1098909696 | bytes 36192256 | tf_op jit(solution)/shard_map/sub | solution.py:50
  92.2 19.0 %fusion.8 = bf16[8,512,2048]{2,1,0:T(8,128)(2,1)} fusion(f32[8,512,2048]{2,1,0:T(8,128)} %get-tuple-element.29, f32[8,512]{1,0:T(8,128)S(1)} %get-tuple-element.28), kind=kLoop, calls=%fused_computation.15 | loop fusion | flops 16777216 | bytes 50348032 | tf_op jit(solution)/shard_map/convert_element_type | solution.py:53
  111.3 13.0 %multiply_reduce_fusion.2 = (f32[512,8]{0,1:T(8,128)}, bf16[8,64,512]{2,1,0:T(8,128)(2,1)}) fusion(bf16[512,512]{0,1:T(8,128)(2,1)S(1)} %convolution_convert_fusion.1, bf16[2048,8,64]{0,2,1:T(8,128)(2,1)} %bitcast.73, bf16[8,512,2048]{2,1,0:T(8,128)(2,1)} %fusion.8), kind=kOutput, calls=%fused_computation.49 | convolution fusion | flops 1075048448 | bytes 19939328 | tf_op jit(solution)/shard_map/hij,jhe->ihe/dot_general | solution.py:55
  124.3 10.8 %fusion.40 = f32[8,64,2048]{2,1,0:T(8,128)} fusion(bf16[512,8,64]{0,2,1:T(8,128)(2,1)S(1)} %bitcast.77, bf16[8,512,2048]{2,1,0:T(8,128)(2,1)} %fusion.8), kind=kOutput, calls=%fused_computation.70 | convolution fusion | flops 1073741824 | bytes 21495808 | tf_op jit(solution)/shard_map/hij,ihe->jhe/dot_general | solution.py:81
  135.1 13.4 %multiply_convert_fusion = bf16[8,512,2048]{2,1,0:T(8,128)(2,1)S(1)} fusion(bf16[512,8,64]{0,2,1:T(8,128)(2,1)S(1)} %bitcast.78, bf16[2048,8,64]{0,2,1:T(8,128)(2,1)} %bitcast.74, f32[8,512]{1,0:T(8,128)} %bitcast.85, f32[8,512,2048]{2,1,0:T(8,128)} %get-tuple-element.29, f32[8,512]{1,0:T(8,128)S(1)} %get-tuple-element.28), kind=kOutput, calls=%fused_computation.5 | convolution fusion | flops 1115684864 | bytes 52985856 | tf_op jit(solution)/shard_map/ihe,jhe->hij/dot_general | solution.py:72
  148.5 7.0 %fusion.39 = f32[8,64,2048]{2,1,0:T(8,128)} fusion(bf16[512,8,64]{0,2,1:T(8,128)(2,1)} %bitcast.81, bf16[8,512,2048]{2,1,0:T(8,128)(2,1)S(1)} %multiply_convert_fusion), kind=kOutput, calls=%fused_computation.69 | convolution fusion | flops 1073741824 | bytes 21495808 | tf_op jit(solution)/shard_map/hij,ihe->jhe/dot_general | solution.py:80
  155.5 0.0 copy-done.2
  155.5 7.8 %pad_maximum_fusion = f32[2048,1024]{0,1:T(8,128)} fusion(f32[2048,512]{0,1:T(8,128)} %bitcast.69, f32[2048,512]{0,1:T(8,128)} %bitcast.70), kind=kLoop, calls=%fused_computation.25 | loop fusion | flops 2097152 | bytes 16777216 | tf_op jit(solution)/shard_map/concatenate | solution.py:83
  163.3 0.7 copy-done.14
  164.0 0.1 reshape.105
  164.1 0.3 copy-done.1
  164.3 5.1 gather_fusion
  169.4 9.2 %all-to-all-start = ((bf16[32,32,512]{2,1,0:T(8,128)(2,1)}), bf16[32,32,512]{2,1,0:T(8,128)(2,1)}, u32[]{:S(2)}, u32[]{:S(2)}) async-start(bf16[32,32,512]{2,1,0:T(8,128)(2,1)} %bitcast.79), calls=%async_computation | async-start | bytes 2097152 | tf_op jit(solution)/shard_map/all_to_all | solution.py:28
  178.7 0.2 all-reduce.3.cloned.1.call-start
  178.9 1.1 convert_element_type.58
  180.0 0.8 copy.29
  180.8 0.1 copy.25
  181.0 0.2 reshape.113
  181.2 0.1 copy.24
  181.3 1.1 reshape.121
  182.4 1.4 fusion.38
  183.8 25.8 %all-to-all-done = bf16[32,32,512]{2,1,0:T(8,128)(2,1)} async-done(((bf16[32,32,512]{2,1,0:T(8,128)(2,1)}), bf16[32,32,512]{2,1,0:T(8,128)(2,1)}, u32[]{:S(2)}, u32[]{:S(2)}) %all-to-all-start) | async-done | bytes 1048608 | tf_op jit(solution)/shard_map/all_to_all | solution.py:28
  209.6 6.0 %fusion.26 = f32[1536,1024]{1,0:T(8,128)} fusion(bf16[512,1024]{1,0:T(8,128)(2,1)} %param.14, bf16[1024,512]{1,0:T(8,128)(2,1)} %bitcast.2, bf16[512,512]{1,0:T(8,128)(2,1)S(1)} %copy-done.1), kind=kOutput, calls=%fused_computation.50 | convolution fusion | flops 1613758464 | bytes 8912896 | tf_op jit(solution)/shard_map/dot_general | solution.py:32
  215.6 25.1 %gather_fusion.1 = f32[4096,1024]{1,0:T(8,128)} fusion(f32[1536,1024]{1,0:T(8,128)} %fusion.26, s32[4096]{0:T(1024)S(1)} %broadcast_clamp_fusion), kind=kCustom, calls=%fused_computation.1 | custom fusion | bytes 33570816 | tf_op jit(solution)/shard_map/gather | solution.py:33
  240.7 18.9 %fusion.34 = (bf16[512,512]{1,0:T(8,128)(2,1)S(1)}, f32[512,8,512]{2,1,0:T(8,128)}, f32[512,8,512]{2,1,0:T(8,128)}, f32[512,512]{1,0:T(8,128)}) fusion(f32[512,8,1024]{2,1,0:T(8,128)} %bitcast.68, f32[512,512]{1,0:T(8,128)} %fusion.38, f32[512,512]{1,0:T(8,128)} %convert_element_type.58, f32[512,8]{1,0:T(8,128)S(1)} %copy.24), kind=kLoop, calls=%fused_computation.65 | loop fusion | flops 28835840 | bytes 37240832 | tf_op jit(solution)/shard_map/reduce_sum | solution.py:96
  259.6 38.4 %scatter_custom_fusion = f32[1536,1024]{1,0:T(8,128)} fusion(s32[4096]{0:T(1024)S(1)} %reshape.121, f32[512,8,512]{2,1,0:T(8,128)} %get-tuple-element.24, f32[]{:T(128)} %constant.2.clone.1, f32[512,8,512]{2,1,0:T(8,128)} %get-tuple-element.23, f32[]{:T(128)} %constant.7.clone.1), kind=kCustom, calls=%fused_computation.10 | custom fusion | flops 8388608 | bytes 23068680 | tf_op jit(solution)/shard_map/scatter-add | solution.py:98
  298.1 1.4 convolution_bitcast_fusion.1
  299.5 6.2 %fusion.20 = f32[512,1024]{1,0:T(8,128)} fusion(f32[1536,1024]{1,0:T(8,128)} %scatter_custom_fusion, bf16[1024,512]{1,0:T(8,128)(2,1)} %bitcast.2, bf16[512,512]{1,0:T(8,128)(2,1)S(1)} %copy-done.1), kind=kOutput, calls=%fused_computation.36 | convolution fusion | flops 1615331328 | bytes 9961472 | tf_op jit(solution)/shard_map/td,tf->df/dot_general | solution.py:101
  305.8 1.4 fusion.41
  307.2 12.4 %convolution_convert_fusion.2 = bf16[8,64,512]{2,1,0:T(8,128)(2,1)} fusion(bf16[2048,8,64]{0,2,1:T(8,128)(2,1)} %bitcast.72, bf16[8,512,2048]{2,1,0:T(8,128)(2,1)} %copy-done.2), kind=kOutput, calls=%fused_computation.47 | convolution fusion | flops 1074003968 | bytes 19398656 | tf_op jit(solution)/shard_map/hij,jhe->ihe/dot_general | solution.py:76
  319.6 1.7 convert.13
  321.4 1.0 copy-done.10
  322.3 3.7 convolution_bitcast_fusion
  326.0 0.0 all-reduce.3.cloned.1.call-update
  326.0 4.9 fusion.22
  331.0 1.7 copy-done.12
  332.6 1.1 slice.64
  333.8 4.9 all-to-all-start.1
  338.7 0.1 reshape.129
  338.8 2.9 fusion.25
  341.7 2.8 fusion.24
  344.5 1.4 convolution_add_fusion
  346.0 13.1 %all-to-all-done.1 = bf16[32,32,512]{2,1,0:T(8,128)(2,1)} async-done(((bf16[32,32,512]{2,1,0:T(8,128)(2,1)}), bf16[32,32,512]{2,1,0:T(8,128)(2,1)}, u32[]{:S(2)}, u32[]{:S(2)}) %all-to-all-start.1) | async-done | bytes 1048608 | tf_op jit(solution)/shard_map/all_to_all | solution.py:104
  359.0 9.4 %scatter_custom_fusion.1 = f32[512,512]{1,0:T(8,128)} fusion(f32[512,512]{1,0:T(8,128)} %convolution_add_fusion, s32[1024]{0:T(1024)S(1)} %reshape.129, bf16[1024,512]{1,0:T(8,128)(2,1)} %bitcast.26), kind=kCustom, calls=%fused_computation.32 | custom fusion | flops 1048576 | bytes 2097152 | tf_op jit(solution)/shard_map/scatter-add | solution.py:111
  368.4 2.1 convert_element_type.66
  370.6 120.5 %all-reduce.3.cloned.1.call-done = (f32[512,512]{0,1:T(8,128)}, f32[512,1024]{1,0:T(8,128)}, f32[512,1536]{0,1:T(8,128)}, f32[512,512]{1,0:T(8,128)}) async-done(((f32[512,512]{0,1:T(8,128)}, f32[512,1024]{1,0:T(8,128)}, f32[512,1536]{0,1:T(8,128)}, f32[512,512]{1,0:T(8,128)}), (f32[512,512]{0,1:T(8,128)}, f32[512,1024]{1,0:T(8,128)}, f32[512,1536]{0,1:T(8,128)}, ...) | async-done | bytes 7340048 | tf_op jit(solution)/shard_map/psum | solution.py:118
  491.0 2.6 copy.30
  493.6 3.5 copy.31
  497.2 3.2 copy.37
  500.3 1.0 copy.38
  (34 shorter events, 0.1 us)
Async XLA Ops:
  7.2 1.4 copy-start
  7.2 7.8 %copy-start.3 = (bf16[512,512]{1,0:T(8,128)(2,1)S(1)}, bf16[512,512]{1,0:T(8,128)(2,1)}, u32[]{:S(2)}) copy-start(bf16[512,512]{1,0:T(8,128)(2,1)} %param.17) | copy-start | bytes 1572868
  7.2 7.8 %copy-start.5 = (bf16[512,512]{1,0:T(8,128)(2,1)S(1)}, bf16[512,512]{1,0:T(8,128)(2,1)}, u32[]{:S(2)}) copy-start(bf16[512,512]{1,0:T(8,128)(2,1)} %param.16) | copy-start | bytes 1572868
  7.2 56.0 %all-gather.2.cloned.1.call-start = ((), (), s32[]{:S(2)}) async-start(), calls=%async_computation.3 | async-start | bytes 5242880 | tf_op jit(solution)/shard_map/all_gather | solution.py:41
  10.6 1.1 copy-start.9
  12.9 306.7 %reduce-scatter.2.cloned.1.call-start = ((), (), s32[]{:S(2)}) async-start(), calls=%async_computation.4 | async-start | bytes 10485760 | tf_op jit(solution)/shard_map/reduce_scatter | solution.py:82
  67.7 7.9 %copy-start.8 = (bf16[512,512]{0,1:T(8,128)(2,1)S(1)}, bf16[512,512]{0,1:T(8,128)(2,1)}, u32[]{:S(2)}) copy-start(bf16[512,512]{0,1:T(8,128)(2,1)} %copy.27) | copy-start | bytes 1572868
  148.5 7.0 %copy-start.2 = (bf16[8,512,2048]{2,1,0:T(8,128)(2,1)}, bf16[8,512,2048]{2,1,0:T(8,128)(2,1)S(1)}, u32[]{:S(2)}) copy-start(bf16[8,512,2048]{2,1,0:T(8,128)(2,1)S(1)} %multiply_convert_fusion) | copy-start | bytes 50331652
  163.3 0.7 copy-start.14
  163.3 1.1 copy-start.1
  164.3 15.7 %copy-start.13 = (s32[512,8]{0,1:T(8,128)S(1)}, s32[512,8]{0,1:T(8,128)}, u32[]{:S(2)}) copy-start(s32[512,8]{0,1:T(8,128)} %param.11) | copy-start | bytes 49156
  164.3 16.8 %copy-start.15 = (s32[512,8]{0,1:T(8,128)S(1)}, s32[512,8]{0,1:T(8,128)}, u32[]{:S(2)}) copy-start(s32[512,8]{0,1:T(8,128)} %param.12) | copy-start | bytes 49156
  164.3 18.1 %copy-start.6 = (bf16[512,512]{1,0:T(8,128)(2,1)S(1)}, bf16[512,512]{1,0:T(8,128)(2,1)}, u32[]{:S(2)}) copy-start(bf16[512,512]{1,0:T(8,128)(2,1)} %param.13) | copy-start | bytes 1572868
  169.4 40.2 %all-to-all-start = ((bf16[32,32,512]{2,1,0:T(8,128)(2,1)}), bf16[32,32,512]{2,1,0:T(8,128)(2,1)}, u32[]{:S(2)}, u32[]{:S(2)}) async-start(bf16[32,32,512]{2,1,0:T(8,128)(2,1)} %bitcast.79), calls=%async_computation | async-start | bytes 2097152 | tf_op jit(solution)/shard_map/all_to_all | solution.py:28
  178.7 312.4 %all-reduce.3.cloned.1.call-start = ((), (), s32[]{:S(2)}) async-start(), calls=%async_computation.5 | async-start | bytes 14680064 | tf_op jit(solution)/shard_map/psum | solution.py:118
  298.1 7.7 %copy-start.4 = (bf16[8,64,512]{2,1,0:T(8,128)(2,1)S(1)}, bf16[8,64,512]{2,1,0:T(8,128)(2,1)}, u32[]{:S(2)}) copy-start(bf16[8,64,512]{2,1,0:T(8,128)(2,1)} %get-tuple-element.31) | copy-start | bytes 1572868
  321.3 1.0 copy-start.10
  331.0 1.7 copy-start.12
  333.8 25.3 %all-to-all-start.1 = ((bf16[32,32,512]{2,1,0:T(8,128)(2,1)}), bf16[32,32,512]{2,1,0:T(8,128)(2,1)}, u32[]{:S(2)}, u32[]{:S(2)}) async-start(bf16[32,32,512]{2,1,0:T(8,128)(2,1)} %bitcast.80), calls=%async_computation.2 | async-start | bytes 2097152 | tf_op jit(solution)/shard_map/all_to_all | solution.py:104
  338.8 5.7 %copy-start.7 = (bf16[512,512]{1,0:T(8,128)(2,1)S(1)}, bf16[512,512]{1,0:T(8,128)(2,1)}, u32[]{:S(2)}) copy-start(bf16[512,512]{1,0:T(8,128)(2,1)} %param.13) | copy-start | bytes 1572868
  491.0 9.3 %copy-start.11 = (f32[512,512]{1,0:T(8,128)S(1)}, f32[512,512]{1,0:T(8,128)}, u32[]{:S(2)}) copy-start(f32[512,512]{1,0:T(8,128)} %get-tuple-element.37) | copy-start | bytes 3145732
Sparse Core Ops, SparseCore 0:
  13.0 50.1 all-gather.1
  163.4 90.9 reduce-scatter.1
  326.2 164.8 all-reduce.2
where the time goes:
time: 515 us; the launch traced here: 508 us
  waiting for transfers between devices  207 us (40%)
  matrix products  108 us (21%)
  other arithmetic  98.5 us (19%)
  local copies, waits for them, and re-layouts  65.8 us (13%)
  starting transfers between devices  14.4 us (3%)
  between operations  14.2 us (3%)
    psum x1, waiting for transfers between devices, body(): lax.psum((grad_gate_w, grad_source_w, grad_qkv_w, grad_out_w), ('blk', 'd...  120 us
    all_gather x1, waiting for transfers between devices, body(): keys_vals = lax.all_gather(qkv[:, feat_width:], 'blk', axis=0, tiled=True)  47.7 us
    scatter-add x1, other arithmetic, body(): jax.ops.segment_sum(edge_terms, neighbour_slots.reshape(-1), num_segments...  38.4 us
    all_to_all x1, waiting for transfers between devices, body(): lax.all_to_all(outgoing, 'dom', split_axis=0, concat_axis=0, tiled=True)  25.8 us
    gather x1, local copies, waits for them, and re-layouts, body(): edge_source = source_terms[neighbour_slots]  25.1 us
    convert_element_type x1, other arithmetic, body(): prob_half = prob_weights.astype(jnp.bfloat16)  19 us
    reduce_sum x1, other arithmetic, body(): d_gate = jnp.sum(d_edge_logit, axis=1).astype(jnp.bfloat16)  18.9 us
    unnamed x37, local copies, waits for them, and re-layouts  17.2 us
  transfers between devices with their start and end apart: 5, of which 4 were waited for; matrix products, arithmetic and copies ran while one was open for 29% of the time, Pallas kernels for 0%

commit v1 on v0

--- a/solution.py
+++ b/solution.py
@@ -115,7 +115,8 @@
     feats_grad = (upstream + d_attn_input + d_table[:node_count] + d_gate_input + d_sent).astype(
         jnp.bfloat16
     )
-    weight_sums = lax.psum((grad_gate_w, grad_source_w, grad_qkv_w, grad_out_w), ("blk", "dom"))
+    inner = lax.psum((grad_gate_w, grad_source_w, grad_qkv_w, grad_out_w), "blk")
+    weight_sums = lax.psum(inner, "dom")
     return (layer_out, feats_grad, weight_sums[0], weight_sums[1], weight_sums[2], weight_sums[3])
 
 

time: 515 us -> 908 us (1.76)
  the two profiles are of different devices: /device:TPU:1 before, /device:TPU:0 now
where the time goes in v1:
time: 908 us; the launch traced here: 901 us
  waiting for transfers between devices  595 us (66%)
  matrix products  108 us (12%)
  other arithmetic  98.7 us (11%)
  local copies, waits for them, and re-layouts  66 us (7%)
  starting transfers between devices  19.6 us (2%)
  between operations  14.3 us (2%)
    psum x1, waiting for transfers between devices, body(): weight_sums = lax.psum(inner, 'dom')  360 us
    psum x1, waiting for transfers between devices, body(): lax.psum((grad_gate_w, grad_source_w, grad_qkv_w, grad_out_w), 'blk')  137 us
    all_gather x1, waiting for transfers between devices, body(): keys_vals = lax.all_gather(qkv[:, feat_width:], 'blk', axis=0, tiled=True)  46 us
    scatter-add x1, other arithmetic, body(): jax.ops.segment_sum(edge_terms, neighbour_slots.reshape(-1), num_segments...  38.4 us
    all_to_all x1, waiting for transfers between devices, body(): lax.all_to_all(outgoing, 'dom', split_axis=0, concat_axis=0, tiled=True)  26.6 us
    gather x1, local copies, waits for them, and re-layouts, body(): edge_source = source_terms[neighbour_slots]  25.3 us
    all_to_all x1, waiting for transfers between devices, body(): lax.all_to_all(d_table[node_count:].reshape(peer_count, -1, feat_width).a...  24.6 us
    reduce_sum x1, other arithmetic, body(): d_gate = jnp.sum(d_edge_logit, axis=1).astype(jnp.bfloat16)  19.1 us
  transfers between devices with their start and end apart: 6, of which 5 were waited for; matrix products, arithmetic and copies ran while one was open for 16% of the time, Pallas kernels for 0%

profile of v1, /device:TPU:0, one launch (start us, length us, event | category | flops | bytes accessed | tf_op | source)
XLA Modules:
  0.0 901.5 jit_solution(4384794739019038468)
XLA Ops:
  7.2 0.0 all-gather.2.cloned.1.call-start
  7.2 1.3 copy-done
  8.6 2.0 convolution_convert_fusion
  10.6 1.1 copy-done.9
  11.8 1.1 slice.39
  12.8 0.0 all-gather.2.cloned.1.call-update
  12.9 0.0 reduce-scatter.2.cloned.1.call-start
  12.9 1.1 slice.41
  14.0 1.0 copy.27
  15.0 0.5 convolution_convert_fusion.1
  15.5 46.0 %all-gather.2.cloned.1.call-done = bf16[2048,1024]{1,0:T(8,128)(2,1)} async-done(((bf16[512,1024]{1,0:T(8,128)(2,1)}), bf16[2048,1024]{1,0:T(8,128)(2,1)}) %all-gather.2.cloned.1.call-update) | async-done | bytes 4194320 | tf_op jit(solution)/shard_map/all_gather | solution.py:41
  61.5 4.5 fusion.36
  66.0 4.0 copy.28
  70.0 3.9 copy.26
  73.9 16.6 %fusion.37 = (f32[8,512]{1,0:T(8,128)S(1)}, f32[8,512,2048]{2,1,0:T(8,128)}) fusion(bf16[512,8,64]{0,2,1:T(8,128)(2,1)S(1)} %bitcast.82, bf16[2048,8,64]{0,2,1:T(8,128)(2,1)} %bitcast.71), kind=kOutput, calls=%fused_computation.67 | convolution fusion | flops 1098909696 | bytes 36192256 | tf_op jit(solution)/shard_map/sub | solution.py:50
  90.5 19.0 %fusion.8 = bf16[8,512,2048]{2,1,0:T(8,128)(2,1)} fusion(f32[8,512,2048]{2,1,0:T(8,128)} %get-tuple-element.33, f32[8,512]{1,0:T(8,128)S(1)} %get-tuple-element.32), kind=kLoop, calls=%fused_computation.15 | loop fusion | flops 16777216 | bytes 50348032 | tf_op jit(solution)/shard_map/convert_element_type | solution.py:53
  109.6 13.0 %multiply_reduce_fusion.2 = (f32[512,8]{0,1:T(8,128)}, bf16[8,64,512]{2,1,0:T(8,128)(2,1)}) fusion(bf16[512,512]{0,1:T(8,128)(2,1)S(1)} %convolution_convert_fusion.1, bf16[2048,8,64]{0,2,1:T(8,128)(2,1)} %bitcast.73, bf16[8,512,2048]{2,1,0:T(8,128)(2,1)} %fusion.8), kind=kOutput, calls=%fused_computation.49 | convolution fusion | flops 1075048448 | bytes 19939328 | tf_op jit(solution)/shard_map/hij,jhe->ihe/dot_general | solution.py:55
  122.6 10.8 %fusion.40 = f32[8,64,2048]{2,1,0:T(8,128)} fusion(bf16[512,8,64]{0,2,1:T(8,128)(2,1)S(1)} %bitcast.77, bf16[8,512,2048]{2,1,0:T(8,128)(2,1)} %fusion.8), kind=kOutput, calls=%fused_computation.70 | convolution fusion | flops 1073741824 | bytes 21495808 | tf_op jit(solution)/shard_map/hij,ihe->jhe/dot_general | solution.py:81
  133.4 13.4 %multiply_convert_fusion = bf16[8,512,2048]{2,1,0:T(8,128)(2,1)S(1)} fusion(bf16[512,8,64]{0,2,1:T(8,128)(2,1)S(1)} %bitcast.78, bf16[2048,8,64]{0,2,1:T(8,128)(2,1)} %bitcast.74, f32[8,512]{1,0:T(8,128)} %bitcast.85, f32[8,512,2048]{2,1,0:T(8,128)} %get-tuple-element.33, f32[8,512]{1,0:T(8,128)S(1)} %get-tuple-element.32), kind=kOutput, calls=%fused_computation.5 | convolution fusion | flops 1115684864 | bytes 52985856 | tf_op jit(solution)/shard_map/ihe,jhe->hij/dot_general | solution.py:72
  146.8 7.0 fusion.39
  153.8 7.8 pad_maximum_fusion
  161.6 0.7 copy-done.14
  162.3 0.1 reshape.105
  162.4 0.3 copy-done.1
  162.6 5.1 gather_fusion
  167.7 9.5 %all-to-all-start = ((bf16[32,32,512]{2,1,0:T(8,128)(2,1)}), bf16[32,32,512]{2,1,0:T(8,128)(2,1)}, u32[]{:S(2)}, u32[]{:S(2)}) async-start(bf16[32,32,512]{2,1,0:T(8,128)(2,1)} %bitcast.79), calls=%async_computation | async-start | bytes 2097152 | tf_op jit(solution)/shard_map/all_to_all | solution.py:28
  177.3 0.2 all-reduce.7.cloned.1.call-start
  177.5 1.1 convert_element_type.58
  178.6 0.8 copy.29
  179.4 0.1 copy.25
  179.6 0.2 reshape.113
  179.8 0.1 copy.24
  179.9 1.1 reshape.121
  181.0 1.4 fusion.38
  182.4 26.6 %all-to-all-done = bf16[32,32,512]{2,1,0:T(8,128)(2,1)} async-done(((bf16[32,32,512]{2,1,0:T(8,128)(2,1)}), bf16[32,32,512]{2,1,0:T(8,128)(2,1)}, u32[]{:S(2)}, u32[]{:S(2)}) %all-to-all-start) | async-done | bytes 1048608 | tf_op jit(solution)/shard_map/all_to_all | solution.py:28
  209.0 6.1 fusion.26
  215.1 25.3 %gather_fusion.1 = f32[4096,1024]{1,0:T(8,128)} fusion(f32[1536,1024]{1,0:T(8,128)} %fusion.26, s32[4096]{0:T(1024)S(1)} %broadcast_clamp_fusion), kind=kCustom, calls=%fused_computation.1 | custom fusion | bytes 33570816 | tf_op jit(solution)/shard_map/gather | solution.py:33
  240.4 19.1 %fusion.34 = (bf16[512,512]{1,0:T(8,128)(2,1)S(1)}, f32[512,8,512]{2,1,0:T(8,128)}, f32[512,8,512]{2,1,0:T(8,128)}, f32[512,512]{1,0:T(8,128)}) fusion(f32[512,8,1024]{2,1,0:T(8,128)} %bitcast.68, f32[512,512]{1,0:T(8,128)} %fusion.38, f32[512,512]{1,0:T(8,128)} %convert_element_type.58, f32[512,8]{1,0:T(8,128)S(1)} %copy.24), kind=kLoop, calls=%fused_computation.65 | loop fusion | flops 28835840 | bytes 37240832 | tf_op jit(solution)/shard_map/reduce_sum | solution.py:96
  259.5 38.4 %scatter_custom_fusion = f32[1536,1024]{1,0:T(8,128)} fusion(s32[4096]{0:T(1024)S(1)} %reshape.121, f32[512,8,512]{2,1,0:T(8,128)} %get-tuple-element.28, f32[]{:T(128)} %constant.2.clone.1, f32[512,8,512]{2,1,0:T(8,128)} %get-tuple-element.27, f32[]{:T(128)} %constant.7.clone.1), kind=kCustom, calls=%fused_computation.10 | custom fusion | flops 8388608 | bytes 23068680 | tf_op jit(solution)/shard_map/scatter-add | solution.py:98
  298.0 1.5 convolution_bitcast_fusion.1
  299.4 6.2 fusion.20
  305.7 1.4 fusion.41
  307.1 12.4 %convolution_convert_fusion.2 = bf16[8,64,512]{2,1,0:T(8,128)(2,1)} fusion(bf16[2048,8,64]{0,2,1:T(8,128)(2,1)} %bitcast.72, bf16[8,512,2048]{2,1,0:T(8,128)(2,1)} %copy-done.2), kind=kOutput, calls=%fused_computation.47 | convolution fusion | flops 1074003968 | bytes 19398656 | tf_op jit(solution)/shard_map/hij,jhe->ihe/dot_general | solution.py:76
  319.5 1.7 convert.13
  321.2 1.0 copy-done.10
  322.2 3.7 convolution_bitcast_fusion
  325.9 0.0 all-reduce.5.cloned.1.call-start
  326.0 137.5 %all-reduce.7.cloned.1.call-done = (f32[512,512]{0,1:T(8,128)}, f32[512,1024]{1,0:T(8,128)}, f32[512,1536]{0,1:T(8,128)}, f32[512,512]{1,0:T(8,128)}) async-done(((f32[512,512]{0,1:T(8,128)}, f32[512,1024]{1,0:T(8,128)}, f32[512,1536]{0,1:T(8,128)}, f32[512,512]{1,0:T(8,128)}), (f32[512,512]{0,1:T(8,128)}, f32[512,1024]{1,0:T(8,128)}, f32[512,1536]{0,1:T(8,128)}, ...) | async-done | bytes 7340048 | tf_op jit(solution)/shard_map/psum | solution.py:118
  463.5 4.9 fusion.22
  468.4 1.7 copy-done.12
  470.1 1.1 slice.64
  471.2 9.8 %all-to-all-start.1 = ((bf16[32,32,512]{2,1,0:T(8,128)(2,1)}), bf16[32,32,512]{2,1,0:T(8,128)(2,1)}, u32[]{:S(2)}, u32[]{:S(2)}) async-start(bf16[32,32,512]{2,1,0:T(8,128)(2,1)} %bitcast.80), calls=%async_computation.2 | async-start | bytes 2097152 | tf_op jit(solution)/shard_map/all_to_all | solution.py:104
  480.9 0.1 reshape.129
  481.0 2.9 fusion.25
  483.9 2.7 fusion.24
  486.6 1.4 convolution_add_fusion
  488.1 24.6 %all-to-all-done.1 = bf16[32,32,512]{2,1,0:T(8,128)(2,1)} async-done(((bf16[32,32,512]{2,1,0:T(8,128)(2,1)}), bf16[32,32,512]{2,1,0:T(8,128)(2,1)}, u32[]{:S(2)}, u32[]{:S(2)}) %all-to-all-start.1) | async-done | bytes 1048608 | tf_op jit(solution)/shard_map/all_to_all | solution.py:104
  512.7 9.4 %scatter_custom_fusion.1 = f32[512,512]{1,0:T(8,128)} fusion(f32[512,512]{1,0:T(8,128)} %convolution_add_fusion, s32[1024]{0:T(1024)S(1)} %reshape.129, bf16[1024,512]{1,0:T(8,128)(2,1)} %bitcast.26), kind=kCustom, calls=%fused_computation.32 | custom fusion | flops 1048576 | bytes 2097152 | tf_op jit(solution)/shard_map/scatter-add | solution.py:111
  522.1 2.1 convert_element_type.66
  524.1 360.3 %all-reduce.5.cloned.1.call-done = (f32[512,512]{0,1:T(8,128)}, f32[512,1024]{1,0:T(8,128)}, f32[512,1536]{0,1:T(8,128)}, f32[512,512]{1,0:T(8,128)}) async-done(((f32[512,512]{0,1:T(8,128)}, f32[512,1024]{1,0:T(8,128)}, f32[512,1536]{0,1:T(8,128)}, f32[512,512]{1,0:T(8,128)}), (f32[512,512]{0,1:T(8,128)}, f32[512,1024]{1,0:T(8,128)}, f32[512,1536]{0,1:T(8,128)}, ...) | async-done | bytes 7340048 | tf_op jit(solution)/shard_map/psum | solution.py:119
  884.4 2.6 copy.30
  887.0 3.5 copy.31
  890.6 3.2 copy.41
  893.7 1.0 copy.42
  (37 shorter events, 0.2 us)
Async XLA Ops:
  7.2 1.4 copy-start
  7.2 7.8 copy-start.3
  7.2 7.8 copy-start.5
  7.2 54.3 %all-gather.2.cloned.1.call-start = ((), (), s32[]{:S(2)}) async-start(), calls=%async_computation.3 | async-start | bytes 5242880 | tf_op jit(solution)/shard_map/all_gather | solution.py:41
  10.6 1.1 copy-start.9
  12.9 306.6 %reduce-scatter.2.cloned.1.call-start = ((), (), s32[]{:S(2)}) async-start(), calls=%async_computation.4 | async-start | bytes 10485760 | tf_op jit(solution)/shard_map/reduce_scatter | solution.py:82
  66.0 7.9 copy-start.8
  146.8 7.0 copy-start.2
  161.6 0.7 copy-start.14
  161.6 1.1 copy-start.1
  162.6 15.9 %copy-start.13 = (s32[512,8]{0,1:T(8,128)S(1)}, s32[512,8]{0,1:T(8,128)}, u32[]{:S(2)}) copy-start(s32[512,8]{0,1:T(8,128)} %param.11) | copy-start | bytes 49156
  162.6 17.1 %copy-start.15 = (s32[512,8]{0,1:T(8,128)S(1)}, s32[512,8]{0,1:T(8,128)}, u32[]{:S(2)}) copy-start(s32[512,8]{0,1:T(8,128)} %param.12) | copy-start | bytes 49156
  162.6 18.4 %copy-start.6 = (bf16[512,512]{1,0:T(8,128)(2,1)S(1)}, bf16[512,512]{1,0:T(8,128)(2,1)}, u32[]{:S(2)}) copy-start(bf16[512,512]{1,0:T(8,128)(2,1)} %param.13) | copy-start | bytes 1572868
  167.7 41.3 %all-to-all-start = ((bf16[32,32,512]{2,1,0:T(8,128)(2,1)}), bf16[32,32,512]{2,1,0:T(8,128)(2,1)}, u32[]{:S(2)}, u32[]{:S(2)}) async-start(bf16[32,32,512]{2,1,0:T(8,128)(2,1)} %bitcast.79), calls=%async_computation | async-start | bytes 2097152 | tf_op jit(solution)/shard_map/all_to_all | solution.py:28
  177.3 286.2 %all-reduce.7.cloned.1.call-start = ((), (), s32[]{:S(2)}) async-start(), calls=%async_computation.6 | async-start | bytes 14680064 | tf_op jit(solution)/shard_map/psum | solution.py:118
  297.9 7.7 copy-start.4
  321.2 1.0 copy-start.10
  325.9 558.5 %all-reduce.5.cloned.1.call-start = ((), (), s32[]{:S(2)}) async-start(), calls=%async_computation.5 | async-start | bytes 14680064 | tf_op jit(solution)/shard_map/psum | solution.py:119
  468.4 1.7 copy-start.12
  471.2 41.5 %all-to-all-start.1 = ((bf16[32,32,512]{2,1,0:T(8,128)(2,1)}), bf16[32,32,512]{2,1,0:T(8,128)(2,1)}, u32[]{:S(2)}, u32[]{:S(2)}) async-start(bf16[32,32,512]{2,1,0:T(8,128)(2,1)} %bitcast.80), calls=%async_computation.2 | async-start | bytes 2097152 | tf_op jit(solution)/shard_map/all_to_all | solution.py:104
  481.0 5.6 copy-start.7
  884.4 9.3 %copy-start.11 = (f32[512,512]{1,0:T(8,128)S(1)}, f32[512,512]{1,0:T(8,128)}, u32[]{:S(2)}) copy-start(f32[512,512]{1,0:T(8,128)} %get-tuple-element.41) | copy-start | bytes 3145732
Sparse Core Ops, SparseCore 0:
  13.0 48.4 all-gather.1
  161.7 91.6 reduce-scatter.1
  326.0 137.3 all-reduce.6
  466.1 418.2 all-reduce.4
